TPU v7x, 512 devices: a whole 4x8x8 slice. The times are simulated.
512 devices in a mesh: vocab: 128 (over z, y, core), dp: 4 (over x).
Axes of the slice: x: 4, y: 8, z: 8, core: 2. Of those that a mesh axis runs over, the one named last changes fastest.
Arguments:
- teacher_hidden: bfloat16 [512, 4096], P(None, ('dp', 'vocab')), may hold values from -2200 to 2200
- student_hidden: bfloat16 [512, 4096], P(None, ('dp', 'vocab')), may hold values from -360 to 360
- teacher_head: bfloat16 [4096, 81920], P('dp', 'vocab'), may hold values from -0.09375 to 0.09375
- student_head: bfloat16 [4096, 81920], P('dp', 'vocab'), may hold values from -0.09375 to 0.09375
- token_ids: int32 [512], P('dp'), may hold values from 0 to 81919
- row_mask: int32 [512], P('dp'), may hold values from 0 to 1
Outputs:
- token_logprob: float32 [512], P('dp')
- loss: float32 [], replicated
- hidden_grad: bfloat16 [512, 4096], P(None, ('dp', 'vocab'))
- head_grad: bfloat16 [4096, 81920], P('dp', 'vocab')
All inputs are finite; a program needn't handle non-finite values.
Results may differ from a plain program's by a relative error of at most 0.012.
Values may be sent and summed in bfloat16 or wider, within the bound.
A program may use at most 64 MiB of HBM per device.

v0:
```python
import jax
import jax.numpy as jnp
from jax import lax
from jax.sharding import PartitionSpec as P


def shards(teacher_hidden, student_hidden, teacher_head, student_head, token_ids, row_mask):
    own_count = token_ids.shape[0]
    voc_width = teacher_head.shape[1]
    teacher_quarter, student_quarter = (
        lax.all_gather(teacher_hidden, "vocab", axis=1, tiled=True),
        lax.all_gather(student_hidden, "vocab", axis=1, tiled=True),
    )
    teacher_own, student_own = (
        lax.all_to_all(teacher_quarter, "dp", split_axis=0, concat_axis=1, tiled=True),
        lax.all_to_all(student_quarter, "dp", split_axis=0, concat_axis=1, tiled=True),
    )
    teacher_logits = jnp.dot(
        teacher_own,
        lax.all_gather(teacher_head, "dp", axis=0, tiled=True),
        preferred_element_type=jnp.float32,
    )
    student_logits = jnp.dot(
        student_own,
        lax.all_gather(student_head, "dp", axis=0, tiled=True),
        preferred_element_type=jnp.float32,
    )
    teacher_max = jnp.max(teacher_logits, axis=1)
    student_max = jnp.max(student_logits, axis=1)
    teacher_top, student_top = lax.pmax((teacher_max, student_max), "vocab")
    teacher_sum = jnp.sum(jnp.exp(teacher_logits - teacher_top[:, None]), axis=1)
    student_sum = jnp.sum(jnp.exp(student_logits - student_top[:, None]), axis=1)
    teacher_total, student_total = lax.psum((teacher_sum, student_sum), "vocab")
    teacher_lse = teacher_top + jnp.log(teacher_total)
    student_lse = student_top + jnp.log(student_total)
    student_logp = student_logits - student_lse[:, None]
    teacher_logp = teacher_logits - teacher_lse[:, None]
    probs = jnp.exp(student_logp)
    gap = student_logp - teacher_logp
    local_ids = token_ids - lax.axis_index("vocab") * voc_width
    is_label = jnp.arange(voc_width, dtype=jnp.int32)[None, :] == local_ids[:, None]
    label_part = jnp.sum(jnp.where(is_label, student_logp, 0.0), axis=1)
    kl_part = jnp.sum(probs * gap, axis=1)
    row_kl, token_logprob = lax.psum((kl_part, label_part), "vocab")
    weights = row_mask.astype(jnp.float32)
    total_rows = own_count * lax.axis_size("dp")
    loss = lax.psum(jnp.sum(weights * row_kl) / total_rows, "dp")
    logit_grad = (weights[:, None] * probs * (gap - row_kl[:, None])).astype(jnp.bfloat16)
    grad_all = lax.all_gather(logit_grad, "dp", axis=0, tiled=True)
    head_grad = lax.dot_general(
        student_quarter, grad_all, (((0,), (0,)), ((), ())), preferred_element_type=jnp.float32
    ).astype(jnp.bfloat16)
    hidden_terms = lax.dot_general(
        grad_all, student_head, (((1,), (1,)), ((), ())), preferred_element_type=jnp.float32
    )
    hidden_grad = lax.psum_scatter(hidden_terms, "vocab", scatter_dimension=1, tiled=True).astype(
        jnp.bfloat16
    )
    return (token_logprob, loss, hidden_grad, head_grad)


def solution(mesh):
    placed = (
        P(None, ("dp", "vocab")),
        P(None, ("dp", "vocab")),
        P("dp", "vocab"),
        P("dp", "vocab"),
        P("dp"),
        P("dp"),
    )
    return jax.shard_map(
        shards,
        mesh=mesh,
        in_specs=placed,
        out_specs=(P("dp"), P(), P(None, ("dp", "vocab")), P("dp", "vocab")),
        check_vma=False,
    )
```

profile of v0, /device:TPU:1, one launch (start us, length us, event | category | flops | bytes accessed | tf_op | source)
XLA Modules:
  0.0 1259.7 jit_solution(17192407568041209790)
XLA Ops:
  7.2 0.0 all-gather.5.cloned.1.call-start
  7.2 0.7 all-gather.5.cloned.1.call-update
  7.9 0.0 all-gather.9.cloned.1.call-start
  7.9 0.7 all-gather.9.cloned.1.call-update
  8.6 0.0 all-gather.7.cloned.1.call-start
  8.7 0.7 all-gather.7.cloned.1.call-update
  9.4 0.0 all-gather.11.cloned.1.call-start
  9.4 0.5 all-gather.11.cloned.1.call-update
  10.0 86.3 %all-gather.5.cloned.1.call-done = bf16[512,1024]{0,1:T(8,128)(2,1)} async-done(((bf16[512,8]{0,1:T(8,128)(2,1)}), bf16[512,1024]{0,1:T(8,128)(2,1)}) %all-gather.5.cloned.1.call-update) | async-done | bytes 1048592 | tf_op jit(solution)/shard_map/all_gather | solution.py:12
  96.2 2.3 copy.17
  98.5 4.0 all-to-all-start
  102.4 0.0 copy-start.3
  102.5 0.0 copy-start.2
  102.5 71.7 %all-gather.9.cloned.1.call-done = bf16[512,1024]{0,1:T(8,128)(2,1)} async-done(((bf16[512,8]{0,1:T(8,128)(2,1)}), bf16[512,1024]{0,1:T(8,128)(2,1)}) %all-gather.9.cloned.1.call-update) | async-done | bytes 1048592 | tf_op jit(solution)/shard_map/all_gather | solution.py:11
  174.2 2.3 copy.19
  176.5 0.0 all-to-all-done
  176.5 4.0 all-to-all-start.1
  180.5 0.0 reduce-scatter.2.cloned.1.call-start
  180.5 0.0 copy-done.3
  180.5 0.0 copy-done.2
  180.5 1.3 copy.18
  181.8 16.4 %all-to-all-done.1 = bf16[4,128,1024]{2,1,0:T(8,128)(2,1)S(1)} async-done(((bf16[4,128,1024]{2,1,0:T(8,128)(2,1)}), bf16[4,128,1024]{2,1,0:T(8,128)(2,1)S(1)}, u32[]{:S(2)}, u32[]{:S(2)}) %all-to-all-start.1) | async-done | bytes 1048608 | tf_op jit(solution)/shard_map/all_to_all | solution.py:15
  198.2 0.7 copy.20
  198.9 39.7 %all-gather.7.cloned.1.call-done = bf16[4096,640]{1,0:T(8,128)(2,1)} async-done(((bf16[1024,640]{1,0:T(8,128)(2,1)}), bf16[4096,640]{1,0:T(8,128)(2,1)}) %all-gather.7.cloned.1.call-update) | async-done | bytes 5242896 | tf_op jit(solution)/shard_map/all_gather | solution.py:25
  238.6 3.9 fusion.2
  242.5 56.2 %all-gather.11.cloned.1.call-done = bf16[4096,640]{1,0:T(8,128)(2,1)} async-done(((bf16[1024,640]{1,0:T(8,128)(2,1)}), bf16[4096,640]{1,0:T(8,128)(2,1)}) %all-gather.11.cloned.1.call-update) | async-done | bytes 5242896 | tf_op jit(solution)/shard_map/all_gather | solution.py:20
  298.7 3.6 fusion.1
  302.3 0.0 copy-start
  302.3 248.3 %all-reduce.2 = (f32[128]{0:T(128)S(1)}, f32[128]{0:T(128)S(1)}) all-reduce(f32[128]{0:T(128)S(1)} %get-tuple-element.28, f32[128]{0:T(128)S(1)} %get-tuple-element.30), channel_id=1, replica_groups=mesh['vocab'=128,'dp'=4] {'vocab'}, use_global_device_ids=true, to_apply=%region_7.0 | all-reduce | flops 256 | bytes 2048 | tf_op jit(solution)/shard_map/pmax | solution.py:30
  550.5 0.2 exponential_reduce_fusion
  550.8 251.2 %all-reduce.1 = (f32[128]{0:T(128)S(1)}, f32[128]{0:T(128)S(1)}) all-reduce(f32[128]{0:T(128)S(1)} %get-tuple-element.32, f32[128]{0:T(128)S(1)} %get-tuple-element.33), channel_id=1, replica_groups=mesh['vocab'=128,'dp'=4] {'vocab'}, use_global_device_ids=true, to_apply=%region_9.10 | all-reduce | flops 256 | bytes 2048 | tf_op jit(solution)/shard_map/psum | solution.py:33
  802.0 0.3 multiply_reduce_fusion
  802.3 247.3 %all-reduce = (f32[128]{0:T(128)}, f32[128]{0:T(128)S(1)}) all-reduce(f32[128]{0:T(128)S(1)} %get-tuple-element.21, f32[128]{0:T(128)S(1)} %get-tuple-element.20), channel_id=1, replica_groups=mesh['vocab'=128,'dp'=4] {'vocab'}, use_global_device_ids=true, to_apply=%region_5.0 | all-reduce | flops 256 | bytes 2048 | tf_op jit(solution)/shard_map/psum | solution.py:44
  1049.6 0.2 multiply_convert_fusion
  1049.8 10.2 all_gather.19
  1060.0 0.0 copy-done
  1060.0 2.4 fusion.3
  1062.3 0.0 copy-start.1
  1062.3 0.0 reduce-scatter.2.cloned.1.call-update
  1062.4 0.6 multiply_reduce_fusion.1
  1063.6 8.2 psum.39
  1071.8 0.0 copy-done.1
  1071.8 0.9 fusion
  1072.7 1.4 copy.21
  1074.2 177.6 %reduce-scatter.2.cloned.1.call-done = f32[512,8]{0,1:T(8,128)} async-done(((f32[512,1024]{0,1:T(8,128)}), f32[512,8]{0,1:T(8,128)}) %reduce-scatter.2.cloned.1.call-update) | async-done | bytes 16400 | tf_op jit(solution)/shard_map/reduce_scatter | solution.py:56
  1251.8 1.3 convert_element_type.17
  (4 shorter events, 0.0 us)
Async XLA Ops:
  7.2 89.1 %all-gather.5.cloned.1.call-start = ((), (), s32[]{:S(2)}) async-start(), calls=%async_computation.3 | async-start | bytes 1056768 | tf_op jit(solution)/shard_map/all_gather | solution.py:12
  7.9 166.3 %all-gather.9.cloned.1.call-start = ((), (), s32[]{:S(2)}) async-start(), calls=%async_computation.5 | async-start | bytes 1056768 | tf_op jit(solution)/shard_map/all_gather | solution.py:11
  8.6 229.9 %all-gather.7.cloned.1.call-start = ((), (), s32[]{:S(2)}) async-start(), calls=%async_computation.4 | async-start | bytes 6553600 | tf_op jit(solution)/shard_map/all_gather | solution.py:25
  9.4 289.3 %all-gather.11.cloned.1.call-start = ((), (), s32[]{:S(2)}) async-start(), calls=%async_computation.6 | async-start | bytes 6553600 | tf_op jit(solution)/shard_map/all_gather | solution.py:20
  98.5 78.0 %all-to-all-start = ((bf16[4,128,1024]{2,1,0:T(8,128)(2,1)}), bf16[4,128,1024]{2,1,0:T(8,128)(2,1)S(1)}, u32[]{:S(2)}, u32[]{:S(2)}) async-start(bf16[4,128,1024]{2,1,0:T(8,128)(2,1)} %bitcast), calls=%async_computation | async-start | bytes 2097152 | tf_op jit(solution)/shard_map/all_to_all | solution.py:16
  102.4 78.0 %copy-start.3 = (s32[128]{0:T(128)S(1)}, s32[128]{0:T(128)}, u32[]{:S(2)}) copy-start(s32[128]{0:T(128)} %param.11) | copy-start | bytes 1540
  102.5 78.0 %copy-start.2 = (s32[128]{0:T(128)S(1)}, s32[128]{0:T(128)}, u32[]{:S(2)}) copy-start(s32[128]{0:T(128)} %param.10) | copy-start | bytes 1540
  176.5 21.7 %all-to-all-start.1 = ((bf16[4,128,1024]{2,1,0:T(8,128)(2,1)}), bf16[4,128,1024]{2,1,0:T(8,128)(2,1)S(1)}, u32[]{:S(2)}, u32[]{:S(2)}) async-start(bf16[4,128,1024]{2,1,0:T(8,128)(2,1)} %bitcast.3), calls=%async_computation.1 | async-start | bytes 2097152 | tf_op jit(solution)/shard_map/all_to_all | solution.py:15
  180.5 1071.3 %reduce-scatter.2.cloned.1.call-start = ((), (), s32[]{:S(2)}) async-start(), calls=%async_computation.7 | async-start | bytes 2113536 | tf_op jit(solution)/shard_map/reduce_scatter | solution.py:56
  302.3 757.7 %copy-start = (bf16[1024,640]{1,0:T(8,128)(2,1)S(1)}, bf16[1024,640]{1,0:T(8,128)(2,1)}, u32[]{:S(2)}) copy-start(bf16[1024,640]{1,0:T(8,128)(2,1)} %param.9) | copy-start | bytes 3932164
  1062.3 9.5 copy-start.1
Sparse Core Ops, SparseCore 0:
  11.0 85.1 all-gather.4
  99.2 74.8 all-gather.8
  176.3 62.2 all-gather.6
  240.5 58.0 all-gather.10
  1062.5 189.2 reduce-scatter.1
where the time goes:
time: 1260 us
  blocking collectives  765 us (61%)
  waiting for transfers between devices  450 us (36%)
  between operations  14.5 us (1%)
    psum x1, blocking collectives, shards(): teacher_total, student_total = lax.psum((teacher_sum, student_sum), 'vocab')  251 us
    pmax x1, blocking collectives, shards(): teacher_top, student_top = lax.pmax((teacher_max, student_max), 'vocab')  248 us
    psum x1, blocking collectives, shards(): row_kl, token_logprob = lax.psum((kl_part, label_part), 'vocab')  247 us
    reduce_scatter x1, waiting for transfers between devices, shards(): lax.psum_scatter(hidden_terms, 'vocab', scatter_dimension=1, tiled=True)  178 us
    all_gather x1, waiting for transfers between devices, shards(): lax.all_gather(student_hidden, 'vocab', axis=1, tiled=True)  86.3 us
    all_gather x1, waiting for transfers between devices, shards(): lax.all_gather(teacher_hidden, 'vocab', axis=1, tiled=True)  71.7 us
    all_gather x1, waiting for transfers between devices, shards(): lax.all_gather(teacher_head, 'dp', axis=0, tiled=True)  56.2 us
    all_gather x1, waiting for transfers between devices, shards(): lax.all_gather(student_head, 'dp', axis=0, tiled=True)  39.7 us
  transfers between devices with their start and end apart: 7, of which 6 were waited for; matrix products, arithmetic and copies ran while one was open for 1% of the time, Pallas kernels for 0%

commit v1 on v0

v1 whole, which is shorter than its diff:
```python
import functools

import jax
import jax.numpy as jnp
from jax import lax
from jax.experimental import pallas as pl
from jax.experimental.pallas import tpu as pltpu
from jax.sharding import PartitionSpec as P

F32 = jnp.float32
BF16 = jnp.bfloat16
NX = 4
LANES = 128


def combine(tiles):
    m_t = jnp.max(tiles[:, 0:1], axis=0)
    m_s = jnp.max(tiles[:, 2:3], axis=0)
    scale_t = jnp.exp(tiles[:, 0:1] - m_t[None])
    scale_s = jnp.exp(tiles[:, 2:3] - m_s[None])
    l_t = jnp.sum(tiles[:, 1:2] * scale_t, axis=0)
    l_s = jnp.sum(tiles[:, 3:4] * scale_s, axis=0)
    k_s = jnp.sum(tiles[:, 4:5] * scale_s, axis=0)
    label = jnp.sum(tiles[:, 5:6], axis=0)
    return m_t, l_t, m_s, l_s, k_s, label


def pack(parts):
    return jnp.concatenate(list(parts) + [jnp.zeros((2, LANES), F32)], axis=0)


def kernel(
    n, rows,
    th_ref, sh_ref, wt_hbm, ws_hbm, ids_ref, mask_ref,
    tok_ref, loss_ref, hid_ref, head_ref,
    own, gat, wt, ws, wtt, wst, xt, xs, part, hop, inc, sta, stb, gb, lossb,
    ht, sibr, sb, rb, sc, rc,
    lsem, s1, r1, s2, r2, s3, r3, sx, rx, ssa, rsa, ssb, rsb, sg, rg, sl, rl,
    s4, r4, s5, r5, s6, r6,
):
    width = wt.shape[1]
    v = lax.axis_index("vocab")
    x = lax.axis_index("dp")
    c = lax.rem(v, 2)
    y = lax.rem(v // 2, n)
    z = v // (2 * n)
    sibling = 1 - c

    def dev(zz, yy, cc, xx=None):
        return ((zz * n + yy) * 2 + cc, x if xx is None else xx)

    def remote(src, dst, send, recv, device):
        return pltpu.make_async_remote_copy(
            src_ref=src, dst_ref=dst, send_sem=send, recv_sem=recv,
            device_id=device, device_id_type=pl.DeviceIdType.MESH,
        )

    def each(count, body, start=1):
        lax.fori_loop(start, count, lambda i, carry: (body(i), carry)[1], 0)

    def step(pos, d):
        return lax.rem(pos + d, n)

    load_t = pltpu.make_async_copy(wt_hbm, wt, lsem.at[0])
    load_s = pltpu.make_async_copy(ws_hbm, ws, lsem.at[1])
    load_t.start()
    load_s.start()

    pair = y * 2 + c

    def group_dev(d):
        other = lax.rem(pair + d, 2 * n)
        return dev(z, other // 2, lax.rem(other, 2))

    barrier = pltpu.get_barrier_semaphore()

    def greet(device):
        pl.semaphore_signal(barrier, inc=1, device_id=device, device_id_type=pl.DeviceIdType.MESH)

    each(2 * n, lambda d: greet(group_dev(d)))
    each(n, lambda d: greet(dev(step(z, d), y, c)))
    each(NX, lambda d: greet(dev(z, y, c, lax.rem(x + d, NX))))

    chunk = [lax.rem(x + d, NX) for d in (2, 1, 3, 0)]
    right, left = chunk[1], chunk[2]
    for rel in range(NX):
        lanes = pl.ds(pl.multiple_of(chunk[rel] * LANES, LANES), LANES)
        block = jnp.concatenate([th_ref[:, lanes].astype(F32), sh_ref[:, lanes].astype(F32)], axis=0)
        own[rel] = block.astype(BF16)
    axes = [(z, y) if rel % 2 == 0 else (y, z) for rel in range(NX)]

    def along_p(rel, d):
        return dev(step(z, d), y, c) if rel % 2 == 0 else dev(z, step(y, d), c)

    def along_q(rel, d):
        return dev(z, step(y, d), c) if rel % 2 == 0 else dev(step(z, d), y, c)

    def first(rel, d):
        p, q = axes[rel]
        return remote(own.at[rel], gat.at[rel, c, p, q], s1.at[rel, d], r1.at[rel, d], along_q(rel, d))

    def second(rel, d):
        p, _ = axes[rel]
        return remote(gat.at[rel, c, p], gat.at[rel, c, p], s2.at[rel, d], r2.at[rel, d], along_p(rel, d))

    def swap(rel, d):
        p = lax.rem(axes[rel][0] + n - d, n)
        return remote(gat.at[rel, c, p], gat.at[rel, c, p], s3.at[rel, d], r3.at[rel, d], dev(z, y, sibling))

    pl.semaphore_wait(barrier, (2 * n - 1) + (n - 1) + (NX - 1))

    for rel in range(NX):
        each(n, lambda d: first(rel, d).start())
    for rel in range(NX):
        p, q = axes[rel]
        gat[rel, c, p, q] = own[rel]
    for rel in range(NX):
        each(n, lambda d: first(rel, d).wait_recv())
        each(n, lambda d: second(rel, d).start())
        swap(rel, 0).start()

    load_t.wait()
    load_s.wait()
    ones = (
        lax.broadcasted_iota(jnp.int32, (LANES, LANES), 0) == lax.broadcasted_iota(jnp.int32, (LANES, LANES), 1)
    ).astype(BF16)

    def turn(i):
        at = pl.ds(pl.multiple_of(i * LANES, LANES), LANES)
        for src, dst in ((wt, wtt), (ws, wst)):
            dst[at, :] = lax.dot_general(
                ones, src[:, at], (((1,), (1,)), ((), ())), preferred_element_type=F32
            ).astype(BF16)

    each(width // LANES, turn, 0)

    def logits(rel):
        def arrive(d):
            second(rel, d).wait_recv()
            swap(rel, d).start()

        each(n, arrive)
        each(n, lambda d: swap(rel, d).wait_recv(), 0)

        def place(i):
            a0, a1 = (gat[rel, k, i] if rel % 2 == 0 else gat[rel, k, :, i] for k in range(2))
            a0, a1 = a0.astype(F32), a1.astype(F32)
            at = pl.ds(pl.multiple_of(i * (n * 16), n * 16), n * 16)
            teacher = jnp.stack([a0[:, 0:8], a1[:, 0:8]], axis=1).reshape(n * 16, LANES)
            student = jnp.stack([a0[:, 8:16], a1[:, 8:16]], axis=1).reshape(n * 16, LANES)
            xt[at, :] = teacher.astype(BF16)
            xs[at, rel * LANES : (rel + 1) * LANES] = student.astype(BF16)

        each(n, place, 0)
        part[rel, 0] = jnp.dot(wtt[...], xt[...], preferred_element_type=F32)
        part[rel, 1] = jnp.dot(
            wst[...], xs[:, rel * LANES : (rel + 1) * LANES], preferred_element_type=F32
        )

    def ring(i, src, dst, to):
        return remote(src, dst, sx.at[i], rx.at[i], dev(z, y, c, to))

    x_copies = [
        ring(0, part.at[0, 0], hop.at[0], right),
        ring(1, part.at[0, 1], hop.at[1], left),
        ring(2, part.at[1, 1], inc.at[0, 1], right),
        ring(3, part.at[2, 0], inc.at[1, 0], left),
        ring(4, part.at[1, 0], inc.at[0, 0], right),
        ring(5, part.at[2, 1], inc.at[1, 1], left),
    ]
    logits(0)
    x_copies[0].start()
    x_copies[1].start()
    logits(1)
    x_copies[2].start()
    logits(2)
    x_copies[3].start()
    x_copies[0].wait_recv()
    part[1, 0] = part[1, 0] + hop[0]
    x_copies[4].start()
    x_copies[1].wait_recv()
    part[2, 1] = part[2, 1] + hop[1]
    x_copies[5].start()
    logits(3)
    for i in (2, 3, 4, 5):
        x_copies[i].wait_recv()
    t = part[3, 0] + inc[0, 0] + inc[1, 0]
    s = part[3, 1] + inc[0, 1] + inc[1, 1]

    m_t = jnp.max(t, axis=0, keepdims=True)
    m_s = jnp.max(s, axis=0, keepdims=True)
    l_t = jnp.sum(jnp.exp(t - m_t), axis=0, keepdims=True)
    e_s = jnp.exp(s - m_s)
    l_s = jnp.sum(e_s, axis=0, keepdims=True)
    k_s = jnp.sum(e_s * (s - t), axis=0, keepdims=True)
    is_label = lax.broadcasted_iota(jnp.int32, (width, LANES), 0) == ids_ref[...] - v * width
    label = jnp.sum(jnp.where(is_label, s, 0.0), axis=0, keepdims=True)
    sta[pair] = pack((m_t, l_t, m_s, l_s, k_s, label))

    def stat_a(d):
        return remote(sta.at[pair], sta.at[pair], ssa.at[d], rsa.at[d], group_dev(d))

    def stat_b(d):
        return remote(stb.at[z], stb.at[z], ssb.at[d], rsb.at[d], dev(step(z, d), y, c))

    each(2 * n, lambda d: stat_a(d).start())
    each(2 * n, lambda d: stat_a(d).wait_recv())
    stb[z] = pack(combine(sta[...]))
    each(n, lambda d: stat_b(d).start())
    each(n, lambda d: stat_b(d).wait_recv())
    m_t, l_t, m_s, l_s, k_s, label = combine(stb[...])
    lse_t = m_t + jnp.log(l_t)
    lse_s = m_s + jnp.log(l_s)
    row_kl = k_s / l_s - lse_s + lse_t
    weights = mask_ref[...].astype(F32)
    logp = s - lse_s
    gap = logp - (t - lse_t)
    gb[:, 3 * LANES :] = (weights * jnp.exp(logp) * (gap - row_kl)).astype(BF16)
    tok_ref[...] = label - lse_s

    def slot(i):
        return slice(i * LANES, (i + 1) * LANES)

    half = width // 2
    g_copies = [
        remote(gb.at[:, slot(3)], gb.at[:, slot(2)], sg.at[0], rg.at[0], dev(z, y, c, right)),
        remote(gb.at[:, slot(3)], gb.at[:, slot(1)], sg.at[1], rg.at[1], dev(z, y, c, left)),
        remote(gb.at[0:half, slot(2)], gb.at[0:half, slot(0)], sg.at[2], rg.at[2], dev(z, y, c, right)),
        remote(gb.at[half:, slot(1)], gb.at[half:, slot(0)], sg.at[3], rg.at[3], dev(z, y, c, left)),
    ]
    g_copies[0].start()
    g_copies[1].start()

    def loss_copy(d):
        return remote(lossb.at[x], lossb.at[x], sl.at[d], rl.at[d], dev(z, y, c, lax.rem(x + d, NX)))

    lossb[x] = jnp.broadcast_to(weights * row_kl, (8, LANES))
    each(NX, lambda d: loss_copy(d).start())

    def core_copy(i):
        return remote(ht.at[i, :, sibling], sibr.at[i], s4.at[i], r4.at[i], dev(z, y, sibling))

    def terms(i):
        ht[i] = jnp.dot(ws[...], gb[:, slot(i)], preferred_element_type=F32).reshape(n * n, 2, 8, LANES)
        core_copy(i).start()

    def outer(i, d):
        p, _ = axes[i]
        return remote(sb.at[i, step(p, d)], rb.at[i, p], s5.at[i, d], r5.at[i, d], along_p(i, d))

    def inner(i, d):
        _, q = axes[i]
        return remote(sc.at[i, step(q, d)], rc.at[i, q], s6.at[i, d], r6.at[i, d], along_q(i, d))

    def send_outer(i):
        p, _ = axes[i]
        core_copy(i).wait_recv()
        total = (ht[i, :, c] + sibr[i]).reshape(n, n, 8, LANES)
        for k in range(n):
            piece = total[k] if i % 2 == 0 else total[:, k]
            sb[i, k] = piece.reshape(n * 8, LANES).astype(BF16)
        each(n, lambda d: outer(i, d).start())
        rb[i, p] = sb[i, p]

    def send_inner(i):
        _, q = axes[i]
        each(n, lambda d: outer(i, d).wait_recv())
        sc[i] = jnp.sum(rb[i].astype(F32), axis=0).reshape(n, 8, LANES)
        each(n, lambda d: inner(i, d).start())
        rc[i, q] = sc[i, q]

    def finish(i):
        each(n, lambda d: inner(i, d).wait_recv())
        lanes = pl.ds(pl.multiple_of(chunk[i] * LANES, LANES), LANES)
        hid_ref[:, lanes] = jnp.sum(rc[i], axis=0).astype(BF16)

    terms(3)
    g_copies[0].wait_recv()
    g_copies[2].start()
    g_copies[1].wait_recv()
    g_copies[3].start()
    send_outer(3)
    terms(2)
    terms(1)
    send_outer(2)
    send_outer(1)
    g_copies[2].wait_recv()
    g_copies[3].wait_recv()
    terms(0)
    send_outer(0)
    each(NX, lambda d: loss_copy(d).wait_recv())
    loss = jnp.sum(lossb[:, 0:1].reshape(NX, LANES)) / rows
    loss_ref[...] = jnp.full((8, LANES), loss, F32)
    head_ref[...] = lax.dot_general(
        xs[...], gb[...], (((1,), (1,)), ((), ())), preferred_element_type=F32
    ).astype(BF16)
    for i in (3, 2, 1, 0):
        send_inner(i)
    for i in (3, 2, 1, 0):
        finish(i)

    for rel in range(NX):
        each(n, lambda d: first(rel, d).wait_send())
        each(n, lambda d: second(rel, d).wait_send())
        each(n, lambda d: swap(rel, d).wait_send(), 0)
        core_copy(rel).wait_send()
        each(n, lambda d: outer(rel, d).wait_send())
        each(n, lambda d: inner(rel, d).wait_send())
    for copy in x_copies + g_copies:
        copy.wait_send()
    each(2 * n, lambda d: stat_a(d).wait_send())
    each(n, lambda d: stat_b(d).wait_send())
    each(NX, lambda d: loss_copy(d).wait_send())


def shards(n, teacher_hidden, student_hidden, teacher_head, student_head, token_ids, row_mask):
    rows = teacher_hidden.shape[0]
    depth, width = teacher_head.shape
    vmem = pl.BlockSpec(memory_space=pltpu.VMEM)
    hbm = pl.BlockSpec(memory_space=pl.ANY)
    dma = pltpu.SemaphoreType.DMA
    scratch = [
        pltpu.VMEM((NX, 16, LANES), BF16),
        pltpu.VMEM((NX, 2, n, n, 16, LANES), BF16),
        pltpu.VMEM((depth, width), BF16),
        pltpu.VMEM((depth, width), BF16),
        pltpu.VMEM((width, depth), BF16),
        pltpu.VMEM((width, depth), BF16),
        pltpu.VMEM((depth, LANES), BF16),
        pltpu.VMEM((depth, rows), BF16),
        pltpu.VMEM((NX, 2, width, LANES), F32),
        pltpu.VMEM((2, width, LANES), F32),
        pltpu.VMEM((2, 2, width, LANES), F32),
        pltpu.VMEM((2 * n, 8, LANES), F32),
        pltpu.VMEM((n, 8, LANES), F32),
        pltpu.VMEM((width, rows), BF16),
        pltpu.VMEM((NX, 8, LANES), F32),
        pltpu.VMEM((NX, n * n, 2, 8, LANES), F32),
        pltpu.VMEM((NX, n * n, 8, LANES), F32),
        pltpu.VMEM((NX, n, n * 8, LANES), BF16),
        pltpu.VMEM((NX, n, n * 8, LANES), BF16),
        pltpu.VMEM((NX, n, 8, LANES), F32),
        pltpu.VMEM((NX, n, 8, LANES), F32),
        dma((2,)),
        dma((NX, n)), dma((NX, n)),
        dma((NX, n)), dma((NX, n)),
        dma((NX, n)), dma((NX, n)),
        dma((6,)), dma((6,)),
        dma((2 * n,)), dma((2 * n,)),
        dma((n,)), dma((n,)),
        dma((4,)), dma((4,)),
        dma((NX,)), dma((NX,)),
        dma((NX,)), dma((NX,)),
        dma((NX, n)), dma((NX, n)),
        dma((NX, n)), dma((NX, n)),
    ]
    tok, loss, hidden, head = pl.pallas_call(
        functools.partial(kernel, n, rows),
        out_shape=(
            jax.ShapeDtypeStruct((1, LANES), F32),
            jax.ShapeDtypeStruct((8, LANES), F32),
            jax.ShapeDtypeStruct((8, rows), BF16),
            jax.ShapeDtypeStruct((depth, width), BF16),
        ),
        in_specs=[vmem, vmem, hbm, hbm, vmem, vmem],
        out_specs=(vmem,) * 4,
        scratch_shapes=scratch,
        compiler_params=pltpu.CompilerParams(
            collective_id=0, has_side_effects=True, vmem_limit_bytes=48 * 1024 * 1024
        ),
        cost_estimate=pl.CostEstimate(flops=6 * 10**9, bytes_accessed=5 * 10**6, transcendentals=3 * 10**5),
    )(
        teacher_hidden.T, student_hidden.T, teacher_head, student_head,
        token_ids.reshape(1, LANES), row_mask.reshape(1, LANES),
    )
    return (tok.reshape(LANES), loss[0, 0], hidden.T, head)


def solution(mesh):
    side = int(round((mesh.shape["vocab"] // 2) ** 0.5))
    placed = (
        P(None, ("dp", "vocab")),
        P(None, ("dp", "vocab")),
        P("dp", "vocab"),
        P("dp", "vocab"),
        P("dp"),
        P("dp"),
    )
    return jax.shard_map(
        functools.partial(shards, side),
        mesh=mesh,
        in_specs=placed,
        out_specs=(P("dp"), P(), P(None, ("dp", "vocab")), P("dp", "vocab")),
        check_vma=False,
    )
```

time: 1260 us -> 100 us (0.08)
  blocking collectives: 765 us -> 0 us
  waiting for transfers between devices: 450 us -> 0 us
  Pallas kernels: 0 us -> 91.1 us
  between operations: 14.5 us -> 0.66 us
    psum x3 -> x0, blocking collectives: 507 us -> none  [the longest x1 251 us: shards(): teacher_total, student_total = lax.psum((teacher_sum, student_sum), 'vocab')]
    all_gather x4 -> x0, waiting for transfers between devices: 254 us -> none  [the longest x1 86.3 us: shards(): lax.all_gather(student_hidden, 'vocab', axis=1, tiled=True)]
    pmax x1 -> x0, blocking collectives: 248 us -> none  [shards(): teacher_top, student_top = lax.pmax((teacher_max, student_max), 'vocab')]
    reduce_scatter x1 -> x0, waiting for transfers between devices: 178 us -> none  [shards(): lax.psum_scatter(hidden_terms, 'vocab', scatter_dimension=1, tiled=True)]
    pallas_call x0 -> x1, Pallas kernels: none -> 91.1 us  [shards(): pl.pallas_call(functools.partial(kernel, n, rows), out_shape=(jax.ShapeDt...]
    all_to_all x2 -> x0, waiting for transfers between devices: 16.4 us -> none  [the longest x1 16.4 us: shards(): lax.all_to_all(teacher_quarter, 'dp', split_axis=0, concat_axis=1, tiled=...]
  transfers between devices with their start and end apart: 7 -> 0, of which waited for: 6 -> 0; matrix products, arithmetic and copies ran while one was open for 1% -> 0% of each run, Pallas kernels for 0% -> 0%
where the time goes in v1:
time: 100 us; the launch traced here: 99.8 us
  Pallas kernels  91.1 us (91%)
  local copies, waits for them, and re-layouts  8.01 us (8%)
    pallas_call x1, Pallas kernels, shards(): pl.pallas_call(functools.partial(kernel, n, rows), out_shape=(jax.ShapeDt...  91.1 us
    unnamed x15, local copies, waits for them, and re-layouts  7.49 us

profile of v1, /device:TPU:1, one launch (start us, length us, event | category | flops | bytes accessed | tf_op | source)
XLA Modules:
  0.0 99.8 jit_solution(6546559415566478574)
XLA Ops:
  0.6 0.0 copy-start
  0.6 1.3 %copy-done = bf16[1024,640]{1,0:T(8,128)(2,1)S(1)} copy-done((bf16[1024,640]{1,0:T(8,128)(2,1)S(1)}, bf16[1024,640]{1,0:T(8,128)(2,1)}, u32[]{:S(2)}) %copy-start) | copy-done | bytes 1310744
  1.9 0.0 copy-start.1
  2.0 1.3 %copy-done.1 = bf16[1024,640]{1,0:T(8,128)(2,1)S(1)} copy-done((bf16[1024,640]{1,0:T(8,128)(2,1)S(1)}, bf16[1024,640]{1,0:T(8,128)(2,1)}, u32[]{:S(2)}) %copy-start.1) | copy-done | bytes 1310744
  3.3 0.0 copy-start.2
  3.3 0.7 copy-done.2
  4.0 0.0 copy-start.3
  4.0 0.7 copy-done.3
  4.7 0.0 copy-start.4
  4.7 0.7 copy-done.4
  5.3 0.0 copy-start.5
  5.3 0.7 copy-done.5
  6.0 91.1 %shard_map.93 = (f32[1,128]{1,0:T(1,128)S(1)}, f32[8,128]{1,0:T(8,128)S(1)}, bf16[8,512]{1,0:T(8,128)(2,1)S(1)}, bf16[1024,640]{1,0:T(8,128)(2,1)S(1)}) custom-call(bf16[8,512]{1,0:T(8,128)(2,1)S(1)} %bitcast.8, bf16[8,512]{1,0:T(8,128)(2,1)S(1)} %bitcast.9, bf16[1024,640]{1,0:T(8,128)(2,1)S(1)} %copy-done, bf16[1024,640]{1,0:T(8,128)(2,1)S(1)} %copy-done.1, ...), custom_call_target="tpu_custom_call" | custom-call | flops 6000000000 | bytes 5000000 | tf_op jit(solution)/shard_map/pallas_call | solution.py:357
  97.1 0.5 slice.3
  97.6 0.5 copy.13
  98.1 0.6 copy.14
  98.7 1.1 %copy.15 = bf16[1024,640]{1,0:T(8,128)(2,1)} copy(bf16[1024,640]{1,0:T(8,128)(2,1)S(1)} %get-tuple-element.19) | data formatting | bytes 2621440
Async XLA Ops:
  0.6 1.3 %copy-start = (bf16[1024,640]{1,0:T(8,128)(2,1)S(1)}, bf16[1024,640]{1,0:T(8,128)(2,1)}, u32[]{:S(2)}) copy-start(bf16[1024,640]{1,0:T(8,128)(2,1)} %wt_hbm.1) | copy-start | bytes 3932164
  1.9 1.3 %copy-start.1 = (bf16[1024,640]{1,0:T(8,128)(2,1)S(1)}, bf16[1024,640]{1,0:T(8,128)(2,1)}, u32[]{:S(2)}) copy-start(bf16[1024,640]{1,0:T(8,128)(2,1)} %ws_hbm.1) | copy-start | bytes 3932164
  3.3 0.7 copy-start.2
  4.0 0.7 copy-start.3
  4.7 0.7 copy-start.4
  5.3 0.7 copy-start.5

commit v2 on v1

v2 whole, which is shorter than its diff:
```python
import functools

import jax
import jax.numpy as jnp
from jax import lax
from jax.experimental import pallas as pl
from jax.experimental.pallas import tpu as pltpu
from jax.sharding import PartitionSpec as P

F32 = jnp.float32
BF16 = jnp.bfloat16
NX = 4
LANES = 128


def code(values):
    top = jnp.maximum(jnp.max(jnp.abs(values), axis=0, keepdims=True), 1e-30)
    scaled = values * (32767.0 / top)
    whole = (scaled + jnp.where(scaled >= 0.0, 0.5, -0.5)).astype(jnp.int32)
    return whole.astype(jnp.int16), jnp.broadcast_to(top / 32767.0, (8, LANES))


def decode(coded, scale):
    return coded.astype(jnp.int32).astype(F32) * scale[0:1]


def combine(stats):
    tops, sums, extras = (stats[:, :, i * LANES : (i + 1) * LANES] for i in range(3))
    top = jnp.max(tops, axis=0)
    scale = jnp.exp(tops - top[None])
    return top, jnp.sum(sums * scale, axis=0), jnp.sum(extras * scale, axis=0), jnp.sum(extras, axis=0)


def kernel(
    n, rows,
    th_hbm, sh_hbm, wt_hbm, ws_hbm, ids_hbm, mask_hbm,
    tok_ref, loss_ref, hid_ref, head_ref,
    th_ref, sh_ref, ids_ref, mask_ref,
    own, gat, wt, ws, wtt, wst, xt, xs, part, diff, unit, hop_s, hop_d, hop_u, inc_s, inc_d, inc_u, sta, stb, tta, ttb, gb, grad, coef, lossb,
    ht, sibr, sb, rb, sc, rc,
    lsem, sent, r1, r2, r3, r4, r5, r6, rx, rg, rs,
):
    width = wt.shape[1]
    v = lax.axis_index("vocab")
    x = lax.axis_index("dp")
    c = lax.rem(v, 2)
    y = lax.rem(v // 2, n)
    z = v // (2 * n)
    sibling = 1 - c

    def dev(zz, yy, cc, xx=None):
        return ((zz * n + yy) * 2 + cc, x if xx is None else xx)

    def remote(src, dst, send, recv, device):
        return pltpu.make_async_remote_copy(
            src_ref=src, dst_ref=dst, send_sem=send, recv_sem=recv,
            device_id=device, device_id_type=pl.DeviceIdType.MESH,
        )

    def each(count, body, start=1):
        lax.fori_loop(start, count, lambda i, carry: (body(i), carry)[1], 0)

    def step(pos, d):
        return lax.rem(pos + d, n)

    first_s, second_s, swap_s, core_s, outer_s, inner_s, stat_a_s, stat_b_s, loss_s, g_s, logit_s, diff_s, teacher_a_s, teacher_b_s, coef_s, unit_s = (
        sent.at[i] for i in range(16)
    )

    def await_bytes(view, sem):
        pltpu.make_async_copy(view, view, sem).wait()

    local = [
        pltpu.make_async_copy(src, dst, lsem.at[i])
        for i, (src, dst) in enumerate((
            (th_hbm, th_ref), (sh_hbm, sh_ref), (wt_hbm, wt), (ws_hbm, ws), (ids_hbm, ids_ref), (mask_hbm, mask_ref),
        ))
    ]
    for i in range(6):
        local[i].start()

    pair = y * 2 + c

    def group_dev(d):
        other = lax.rem(pair + d, 2 * n)
        return dev(z, other // 2, lax.rem(other, 2))

    barrier = pltpu.get_barrier_semaphore()

    def greet(device):
        pl.semaphore_signal(barrier, inc=1, device_id=device, device_id_type=pl.DeviceIdType.MESH)

    each(2 * n, lambda d: greet(group_dev(d)))
    each(n, lambda d: greet(dev(step(z, d), y, c)))
    each(NX, lambda d: greet(dev(z, y, c, lax.rem(x + d, NX))))

    chunk = [lax.rem(x + d, NX) for d in (2, 1, 3, 0)]
    right, left = chunk[1], chunk[2]
    local[0].wait()
    local[1].wait()
    for rel in range(NX):
        lanes = pl.ds(pl.multiple_of(chunk[rel] * LANES, LANES), LANES)
        block = jnp.concatenate([th_ref[:, lanes].astype(F32), sh_ref[:, lanes].astype(F32)], axis=0)
        own[rel] = block.astype(BF16)
    flip = c
    p, q = (1 - flip) * z + flip * y, (1 - flip) * y + flip * z

    def along_p(d):
        return dev(step(z, d * (1 - flip)), step(y, d * flip), c)

    def along_q(d):
        return dev(step(z, d * flip), step(y, d * (1 - flip)), c)

    def first(cut, sem, d):
        return remote(own.at[cut], gat.at[cut, c, p, q], first_s, sem, along_q(d))

    def second(rel, sem, d):
        return remote(gat.at[rel, c, p], gat.at[rel, c, p], second_s, r2.at[rel, sem], along_p(d))

    def swap(rel, d):
        at = lax.rem(p + n - d, n)
        return remote(gat.at[rel, c, at], gat.at[rel, c, at], swap_s, r3.at[rel], dev(z, y, sibling))

    pl.semaphore_wait(barrier, (2 * n - 1) + (n - 1) + (NX - 1))

    near = [d for d in range(1, n) if min(d, n - d) <= n // 4]
    far = [d for d in range(1, n) if d not in near]
    lead, rest = slice(0, 1), slice(1, NX)
    each(n, lambda d: first(lead, r1.at[0], d).start())
    each(n, lambda d: first(rest, r1.at[1], d).start())
    for rel in range(NX):
        gat[rel, c, p, q] = own[rel]

    def spread(rel):
        for d in far:
            second(rel, 1, d).start()
        for d in near:
            second(rel, 0, d).start()
        swap(rel, 0).start()

    await_bytes(gat.at[lead, 0, 0, 0 : n - 1], r1.at[0])
    spread(0)
    await_bytes(gat.at[rest, 0, 0, 0 : n - 1], r1.at[1])
    for rel in range(1, NX):
        spread(rel)

    for i in range(2, 6):
        local[i].wait()
    ones = (
        lax.broadcasted_iota(jnp.int32, (LANES, LANES), 0) == lax.broadcasted_iota(jnp.int32, (LANES, LANES), 1)
    ).astype(BF16)

    def turn(i):
        at = pl.ds(pl.multiple_of(i * LANES, LANES), LANES)
        for src, dst in ((wt, wtt), (ws, wst)):
            dst[at, :] = lax.dot_general(
                ones, src[:, at], (((1,), (1,)), ((), ())), preferred_element_type=F32
            ).astype(BF16)

    each(width // LANES, turn, 0)

    half = width // 2
    upper, lower = slice(0, half), slice(half, width)

    def logits(rel, after_student=lambda: None):
        for sem, group in ((0, near), (1, far)):
            if group:
                await_bytes(gat.at[rel, 0, 0 : len(group)], r2.at[rel, sem])
            for d in group:
                swap(rel, d).start()
        await_bytes(gat.at[rel, 0], r3.at[rel])

        def place(i):
            a0, a1 = gat[rel, 0, i].astype(F32), gat[rel, 1, :, i].astype(F32)
            at = pl.ds(pl.multiple_of(i * (n * 16), n * 16), n * 16)
            teacher = jnp.stack([a0[:, 0:8], a1[:, 0:8]], axis=1).reshape(n * 16, LANES)
            student = jnp.stack([a0[:, 8:16], a1[:, 8:16]], axis=1).reshape(n * 16, LANES)
            xt[at, :] = teacher.astype(BF16)
            xs[at, rel * LANES : (rel + 1) * LANES] = student.astype(BF16)

        each(n, place, 0)
        student = jnp.dot(wst[...], xs[:, rel * LANES : (rel + 1) * LANES], preferred_element_type=F32)
        part[rel, 1] = student
        after_student()
        part[rel, 0] = student - jnp.dot(wtt[...], xt[...], preferred_element_type=F32)
        if rel == 0:
            diff[0], unit[0] = code(part[0, 0])
        elif rel < NX - 1:
            early_rows = lower if rel == 1 else upper
            diff[rel, early_rows], unit[rel] = code(part[rel, 0, early_rows])

    def ring(src, dst, send, recv, to):
        return remote(src, dst, send, recv, dev(z, y, c, to))

    def hop_pair(cut, way, to):
        return [
            ring(part.at[0, 1, cut], hop_s.at[way], logit_s, rx.at[way], to),
            ring(unit.at[0], hop_u.at[way], unit_s, rx.at[6 + way], to),
            ring(diff.at[0, cut], hop_d.at[way], diff_s, rx.at[2 + way], to),
        ]

    def last_pair(rel, cut, way, to, unit_at):
        return [
            ring(part.at[rel, 1, cut], inc_s.at[way, cut], logit_s, rx.at[4], to),
            ring(unit.at[unit_at], inc_u.at[way, 0 if cut == upper else 1], unit_s, rx.at[8], to),
            ring(diff.at[rel, cut], inc_d.at[way, cut], diff_s, rx.at[5], to),
        ]

    hops = [hop_pair(upper, 0, right), hop_pair(lower, 1, left)]
    early = [last_pair(1, lower, 0, right, 1), last_pair(2, upper, 1, left, 2)]
    late = [last_pair(1, upper, 0, right, 3), last_pair(2, lower, 1, left, 4)]

    def start(*copies):
        for copy in copies:
            copy.start()

    def add_hop(way, rel, cut):
        hops[way][0].wait_recv()
        part[rel, 1, cut] = part[rel, 1, cut] + hop_s[way]
        late[way][0].start()
        hops[way][1].wait_recv()
        hops[way][2].wait_recv()
        diff[rel, cut], unit[3 + way] = code(part[rel, 0, cut] + decode(hop_d[way], hop_u[way]))
        start(*late[way][1:])

    logits(0, lambda: start(hops[0][0], hops[1][0]))
    start(*hops[0][1:], *hops[1][1:])
    logits(1, lambda: start(early[0][0]))
    start(*early[0][1:])
    logits(2, lambda: start(early[1][0]))
    start(*early[1][1:])
    add_hop(0, 1, upper)
    add_hop(1, 2, lower)
    logits(3)
    await_bytes(inc_s, rx.at[4])
    await_bytes(inc_d, rx.at[5])
    await_bytes(inc_u, rx.at[8])
    s = part[3, 1] + inc_s[0] + inc_s[1]
    gap = jnp.concatenate(
        [
            part[3, 0, cut] + decode(inc_d[0, cut], inc_u[0, k]) + decode(inc_d[1, cut], inc_u[1, k])
            for k, cut in enumerate((upper, lower))
        ],
        axis=0,
    )

    def stat_a(buf, send, sem, d):
        return remote(buf.at[pair], buf.at[pair], send, sem, group_dev(d))

    def stat_b(buf, send, sem, d):
        return remote(buf.at[z], buf.at[z], send, sem, dev(step(z, d), y, c))

    def send_a(buf, send, sem, parts):
        buf[pair] = jnp.concatenate(parts, axis=1)
        each(2 * n, lambda d: stat_a(buf, send, sem, d).start())

    def send_b(buf, send, sem, parts):
        buf[z] = jnp.concatenate(parts, axis=1)
        each(n, lambda d: stat_b(buf, send, sem, d).start())

    def slot(i):
        return slice(i * LANES, (i + 1) * LANES)

    quarter = half // 2
    cuts = [slice(k * quarter, (k + 1) * quarter) for k in range(4)]

    def g_copy(i, part_rows, source, target, to):
        return ring(gb.at[:, part_rows, slot(source)], gb.at[:, part_rows, slot(target)], g_s, rg.at[i], to)

    g_lead = [
        g_copy(0, cuts[0], 3, 2, right),
        g_copy(1, cuts[2], 3, 1, left),
        g_copy(2, cuts[1], 3, 2, right),
        g_copy(3, cuts[3], 3, 1, left),
    ]
    g_rest = [g_copy(4, lower, 3, 2, right), g_copy(5, upper, 3, 1, left)]
    g_relay = [
        g_copy(6, cuts[0], 2, 0, right),
        g_copy(6, cuts[2], 1, 0, left),
        g_copy(6, cuts[1], 2, 0, right),
        g_copy(6, cuts[3], 1, 0, left),
    ]
    m_s = jnp.max(s, axis=0, keepdims=True)
    e_s = jnp.exp(s - m_s)
    l_s = jnp.sum(e_s, axis=0, keepdims=True)
    k_s = jnp.sum(e_s * gap, axis=0, keepdims=True)
    send_a(sta, stat_a_s, rs.at[0], (m_s, l_s, k_s))
    own_top, own_mean = m_s, k_s / l_s
    gb[0, :, slot(3)] = e_s.astype(BF16)
    gb[1, :, slot(3)] = (e_s * (gap - own_mean)).astype(BF16)
    start(*g_lead, *g_rest)
    t = s - gap
    m_t = jnp.max(t, axis=0, keepdims=True)
    l_t = jnp.sum(jnp.exp(t - m_t), axis=0, keepdims=True)
    is_label = lax.broadcasted_iota(jnp.int32, (width, LANES), 0) == ids_ref[...] - v * width
    label = jnp.sum(jnp.where(is_label, s, 0.0), axis=0, keepdims=True)
    send_a(tta, teacher_a_s, rs.at[3], (m_t, l_t, label))
    await_bytes(sta.at[0 : 2 * n - 1], rs.at[0])
    send_b(stb, stat_b_s, rs.at[1], combine(sta[...])[:3])
    for k in range(4):
        g_lead[k].wait_recv()
        g_relay[k].start()
    await_bytes(tta.at[0 : 2 * n - 1], rs.at[3])
    m_t, l_t, _, label = combine(tta[...])
    send_b(ttb, teacher_b_s, rs.at[4], (m_t, l_t, label))
    await_bytes(stb.at[0 : n - 1], rs.at[1])
    m_s, l_s, k_s, _ = combine(stb[...])
    lse_s = m_s + jnp.log(l_s)
    mean_gap = k_s / l_s
    weights = mask_ref[...].astype(F32)
    factor = weights * jnp.exp(own_top - lse_s)
    coef[3] = jnp.concatenate([factor, factor * (mean_gap - own_mean), jnp.zeros((6, LANES), F32)], axis=0)
    coef_copies = [
        ring(coef.at[3], coef.at[0], coef_s, rs.at[5], chunk[0]),
        ring(coef.at[3], coef.at[2], coef_s, rs.at[7], right),
        ring(coef.at[3], coef.at[1], coef_s, rs.at[6], left),
    ]
    start(*coef_copies)

    def gradient(i):
        scale, shift = coef[i, 0:1], coef[i, 1:2]
        grad[:, slot(i)] = (
            scale * gb[1, :, slot(i)].astype(F32) - shift * gb[0, :, slot(i)].astype(F32)
        ).astype(BF16)

    def loss_copy(d):
        return remote(lossb.at[x], lossb.at[x], loss_s, rs.at[2], dev(z, y, c, lax.rem(x + d, NX)))

    def send_loss():
        await_bytes(ttb.at[0 : n - 1], rs.at[4])
        m_t, l_t, _, label = combine(ttb[...])
        tok_ref[...] = label - lse_s
        row_kl = mean_gap - lse_s + m_t + jnp.log(l_t)
        lossb[x] = jnp.broadcast_to(weights * row_kl, (8, LANES))
        each(NX, lambda d: loss_copy(d).start())

    def core_copy(i):
        return remote(ht.at[i, :, sibling], sibr.at[i], core_s, r4.at[i], dev(z, y, sibling))

    def terms(i):
        gradient(i)
        ht[i] = jnp.dot(ws[...], grad[:, slot(i)], preferred_element_type=F32).reshape(n * n, 2, 8, LANES)
        core_copy(i).start()

    def outer(i, d):
        return remote(sb.at[i, step(p, d)], rb.at[i, p], outer_s, r5.at[i], along_p(d))

    def inner(i, d):
        return remote(sc.at[i, step(q, d)], rc.at[i, q], inner_s, r6.at[i], along_q(d))

    def send_outer(i):
        core_copy(i).wait_recv()
        total = (ht[i, :, c] + sibr[i]).reshape(n, n, 8, LANES)
        for k in range(n):
            piece = jnp.where(c == 0, total[k], total[:, k])
            sb[i, k] = piece.reshape(n * 8, LANES).astype(BF16)
        each(n, lambda d: outer(i, d).start())
        rb[i, p] = sb[i, p]

    def send_inner(i):
        await_bytes(rb.at[i, 0 : n - 1], r5.at[i])
        sc[i] = jnp.sum(rb[i].astype(F32), axis=0).reshape(n, 8, LANES)
        each(n, lambda d: inner(i, d).start())
        rc[i, q] = sc[i, q]

    def finish(i):
        await_bytes(rc.at[i, 0 : n - 1], r6.at[i])
        lanes = pl.ds(pl.multiple_of(chunk[i] * LANES, LANES), LANES)
        hid_ref[:, lanes] = jnp.sum(rc[i], axis=0)

    terms(3)
    send_loss()
    send_outer(3)
    g_rest[0].wait_recv()
    coef_copies[1].wait_recv()
    terms(2)
    g_rest[1].wait_recv()
    coef_copies[2].wait_recv()
    terms(1)
    send_outer(2)
    send_outer(1)
    await_bytes(gb.at[:, :, slot(0)], rg.at[6])
    coef_copies[0].wait_recv()
    terms(0)
    send_outer(0)
    await_bytes(lossb.at[0 : NX - 1], rs.at[2])
    loss = jnp.sum(lossb[:, 0:1].reshape(NX, LANES)) / rows
    loss_ref[...] = jnp.full((1, LANES), loss, F32)
    head_ref[...] = lax.dot_general(
        xs[...], grad[...], (((1,), (1,)), ((), ())), preferred_element_type=F32
    ).astype(BF16)
    for i in (3, 2, 1, 0):
        send_inner(i)
    for i in (3, 2, 1, 0):
        finish(i)

    for view, sem in (
        (gat.at[:, 0, 0, 0 : n - 1], first_s),
        (gat.at[:, 0, 0 : n - 1], second_s),
        (gat.at[:, 0], swap_s),
        (sibr, core_s),
        (sb.at[:, 0 : n - 1], outer_s),
        (sc.at[:, 0 : n - 1], inner_s),
        (sta.at[0 : 2 * n - 1], stat_a_s),
        (tta.at[0 : 2 * n - 1], teacher_a_s),
        (stb.at[0 : n - 1], stat_b_s),
        (ttb.at[0 : n - 1], teacher_b_s),
        (lossb.at[0 : NX - 1], loss_s),
        (gb.at[:, :, 0 : 3 * LANES], g_s),
        (coef.at[0 : NX - 1], coef_s),
        (part.at[0 : NX - 1, 1], logit_s),
        (diff, diff_s),
        (unit, unit_s),
    ):
        await_bytes(view, sem)


def store(tok_ref, loss_ref, hid_ref, head_ref, tok_out, loss_out, hid_out, head_out, one, rounded, sems):
    copies = [
        pltpu.make_async_copy(src, dst, sems.at[i])
        for i, (src, dst) in enumerate(
            ((head_ref, head_out), (tok_ref, tok_out), (one, loss_out), (rounded, hid_out))
        )
    ]
    copies[0].start()
    copies[1].start()
    one[...] = loss_ref[:, 0:1]
    rounded[...] = hid_ref[...].astype(BF16)
    copies[2].start()
    copies[3].start()
    for copy in copies:
        copy.wait()


def shards(n, teacher_hidden, student_hidden, teacher_head, student_head, token_ids, row_mask):
    rows = teacher_hidden.shape[0]
    depth, width = teacher_head.shape
    hbm = pl.BlockSpec(memory_space=pl.ANY)
    dma = pltpu.SemaphoreType.DMA
    scratch = [
        pltpu.VMEM((8, rows), BF16),
        pltpu.VMEM((8, rows), BF16),
        pltpu.VMEM((1, LANES), jnp.int32),
        pltpu.VMEM((1, LANES), jnp.int32),
        pltpu.VMEM((NX, 16, LANES), BF16),
        pltpu.VMEM((NX, 2, n, n, 16, LANES), BF16),
        pltpu.VMEM((depth, width), BF16),
        pltpu.VMEM((depth, width), BF16),
        pltpu.VMEM((width, depth), BF16),
        pltpu.VMEM((width, depth), BF16),
        pltpu.VMEM((depth, LANES), BF16),
        pltpu.VMEM((depth, rows), BF16),
        pltpu.VMEM((NX, 2, width, LANES), F32),
        pltpu.VMEM((NX - 1, width, LANES), jnp.int16),
        pltpu.VMEM((6, 8, LANES), F32),
        pltpu.VMEM((2, width // 2, LANES), F32),
        pltpu.VMEM((2, width // 2, LANES), jnp.int16),
        pltpu.VMEM((2, 8, LANES), F32),
        pltpu.VMEM((2, width, LANES), F32),
        pltpu.VMEM((2, width, LANES), jnp.int16),
        pltpu.VMEM((2, 2, 8, LANES), F32),
        pltpu.VMEM((2 * n, 1, 3 * LANES), F32),
        pltpu.VMEM((n, 1, 3 * LANES), F32),
        pltpu.VMEM((2 * n, 1, 3 * LANES), F32),
        pltpu.VMEM((n, 1, 3 * LANES), F32),
        pltpu.VMEM((2, width, rows), BF16),
        pltpu.VMEM((width, rows), BF16),
        pltpu.VMEM((NX, 8, LANES), F32),
        pltpu.VMEM((NX, 8, LANES), F32),
        pltpu.VMEM((NX, n * n, 2, 8, LANES), F32),
        pltpu.VMEM((NX, n * n, 8, LANES), F32),
        pltpu.VMEM((NX, n, n * 8, LANES), BF16),
        pltpu.VMEM((NX, n, n * 8, LANES), BF16),
        pltpu.VMEM((NX, n, 8, LANES), F32),
        pltpu.VMEM((NX, n, 8, LANES), F32),
        dma((6,)), dma((16,)), dma((2,)), dma((NX, 2)), dma((NX,)), dma((NX,)), dma((NX,)), dma((NX,)),
        dma((9,)), dma((7,)), dma((8,)),
    ]
    tok, loss, hidden, head = pl.pallas_call(
        functools.partial(kernel, n, rows),
        out_shape=(
            pltpu.VMEM((1, LANES), F32),
            pltpu.VMEM((1, LANES), F32),
            pltpu.VMEM((8, rows), F32),
            pltpu.VMEM((depth, width), BF16),
        ),
        in_specs=[hbm] * 6,
        out_specs=(pl.BlockSpec(memory_space=pltpu.VMEM),) * 4,
        scratch_shapes=scratch,
        compiler_params=pltpu.CompilerParams(
            collective_id=0, has_side_effects=True, vmem_limit_bytes=60 * 1024 * 1024
        ),
        cost_estimate=pl.CostEstimate(flops=6 * 10**9, bytes_accessed=5 * 10**6, transcendentals=3 * 10**5),
    )(
        teacher_hidden.T, student_hidden.T, teacher_head, student_head,
        token_ids.reshape(1, LANES), row_mask.reshape(1, LANES),
    )
    vmem = pl.BlockSpec(memory_space=pltpu.VMEM)
    tok, loss, hidden, head = pl.pallas_call(
        store,
        out_shape=(
            jax.ShapeDtypeStruct((1, LANES), F32),
            jax.ShapeDtypeStruct((1, 1), F32),
            jax.ShapeDtypeStruct((8, rows), BF16),
            jax.ShapeDtypeStruct((depth, width), BF16),
        ),
        in_specs=[vmem] * 4,
        out_specs=(hbm,) * 4,
        scratch_shapes=[pltpu.VMEM((1, 1), F32), pltpu.VMEM((8, rows), BF16), dma((4,))],
        compiler_params=pltpu.CompilerParams(vmem_limit_bytes=4 * 1024 * 1024),
    )(tok, loss, hidden, head)
    return (tok.reshape(LANES), loss.reshape(()), hidden.T, head)


def solution(mesh):
    side = int(round((mesh.shape["vocab"] // 2) ** 0.5))
    placed = (
        P(None, ("dp", "vocab")),
        P(None, ("dp", "vocab")),
        P("dp", "vocab"),
        P("dp", "vocab"),
        P("dp"),
        P("dp"),
    )
    return jax.shard_map(
        functools.partial(shards, side),
        mesh=mesh,
        in_specs=placed,
        out_specs=(P("dp"), P(), P(None, ("dp", "vocab")), P("dp", "vocab")),
        check_vma=False,
    )
```

time: 100 us -> 77.9 us (0.78)
  Pallas kernels: 91.1 us -> 77.2 us
  local copies, waits for them, and re-layouts: 8.01 us -> 0 us
    pallas_call x1 -> x2, Pallas kernels: 91.1 us -> 77.2 us  [the longest x1 76.1 us: shards(): pl.pallas_call(functools.partial(kernel, n, rows), out_shape=(pltpu.VMEM(...]
    unnamed x15 -> x0, local copies, waits for them, and re-layouts: 7.49 us -> none
where the time goes in v2:
time: 77.9 us; the launch traced here: 77.8 us
  Pallas kernels  77.2 us (99%)
    pallas_call x1, Pallas kernels, shards(): pl.pallas_call(functools.partial(kernel, n, rows), out_shape=(pltpu.VMEM(...  76.1 us

profile of v2, /device:TPU:1, one launch (start us, length us, event | category | flops | bytes accessed | tf_op | source)
XLA Modules:
  0.0 77.8 jit_solution(6706043470158218078)
XLA Ops:
  0.6 76.1 %shard_map.93 = (f32[1,128]{1,0:T(1,128)S(1)}, f32[1,128]{1,0:T(1,128)S(1)}, f32[8,512]{1,0:T(8,128)S(1)}, bf16[1024,640]{1,0:T(8,128)(2,1)S(1)}) custom-call(bf16[8,512]{1,0:T(8,128)(2,1)} %bitcast.7, bf16[8,512]{1,0:T(8,128)(2,1)} %bitcast.8, bf16[1024,640]{1,0:T(8,128)(2,1)} %wt_hbm.1, bf16[1024,640]{1,0:T(8,128)(2,1)} %ws_hbm.1, s32[1,128]{1,0:T(1,128)} %bitcast.10, ...), custom_call_target="tpu_custom_call" | custom-call | flops 6000000000 | bytes 5000000 | tf_op jit(solution)/shard_map/pallas_call | solution.py:479
  76.7 1.1 %shard_map.94 = (f32[1,128]{1,0:T(1,128)}, f32[1,1]{1,0:T(1,128)}, bf16[8,512]{1,0:T(8,128)(2,1)}, bf16[1024,640]{1,0:T(8,128)(2,1)}) custom-call(f32[1,128]{1,0:T(1,128)S(1)} %get-tuple-element.12.tok_ref, f32[1,128]{1,0:T(1,128)S(1)} %get-tuple-element.13.loss_ref, f32[8,512]{1,0:T(8,128)S(1)} %get-tuple-element.14.hid_ref, ...), custom_call_target="tpu_custom_call" | custom-call | tf_op jit(solution)/shard_map/pallas_call | solution.py:499

commit v3 on v2

--- a/solution.py
+++ b/solution.py
@@ -70,6 +70,21 @@
     def await_bytes(view, sem):
         pltpu.make_async_copy(view, view, sem).wait()
 
+    pair = y * 2 + c
+
+    def group_dev(d):
+        other = lax.rem(pair + d, 2 * n)
+        return dev(z, other // 2, lax.rem(other, 2))
+
+    barrier = pltpu.get_barrier_semaphore()
+
+    def greet(device):
+        pl.semaphore_signal(barrier, inc=1, device_id=device, device_id_type=pl.DeviceIdType.MESH)
+
+    each(n, lambda d: greet(dev(step(z, d), y, c)))
+    each(2 * n, lambda d: greet(group_dev(d)))
+    each(NX, lambda d: greet(dev(z, y, c, lax.rem(x + d, NX))))
+
     local = [
         pltpu.make_async_copy(src, dst, lsem.at[i])
         for i, (src, dst) in enumerate((
@@ -78,21 +93,6 @@
     ]
     for i in range(6):
         local[i].start()
-
-    pair = y * 2 + c
-
-    def group_dev(d):
-        other = lax.rem(pair + d, 2 * n)
-        return dev(z, other // 2, lax.rem(other, 2))
-
-    barrier = pltpu.get_barrier_semaphore()
-
-    def greet(device):
-        pl.semaphore_signal(barrier, inc=1, device_id=device, device_id_type=pl.DeviceIdType.MESH)
-
-    each(2 * n, lambda d: greet(group_dev(d)))
-    each(n, lambda d: greet(dev(step(z, d), y, c)))
-    each(NX, lambda d: greet(dev(z, y, c, lax.rem(x + d, NX))))
 
     chunk = [lax.rem(x + d, NX) for d in (2, 1, 3, 0)]
     right, left = chunk[1], chunk[2]
@@ -123,6 +123,21 @@
 
     pl.semaphore_wait(barrier, (2 * n - 1) + (n - 1) + (NX - 1))
 
+    ones = (
+        lax.broadcasted_iota(jnp.int32, (LANES, LANES), 0) == lax.broadcasted_iota(jnp.int32, (LANES, LANES), 1)
+    ).astype(BF16)
+
+    def turn(load, src, dst):
+        local[load].wait()
+
+        def block(i):
+            at = pl.ds(pl.multiple_of(i * LANES, LANES), LANES)
+            dst[at, :] = lax.dot_general(
+                ones, src[:, at], (((1,), (1,)), ((), ())), preferred_element_type=F32
+            ).astype(BF16)
+
+        each(width // LANES, block, 0)
+
     near = [d for d in range(1, n) if min(d, n - d) <= n // 4]
     far = [d for d in range(1, n) if d not in near]
     lead, rest = slice(0, 1), slice(1, NX)
@@ -138,27 +153,16 @@
             second(rel, 0, d).start()
         swap(rel, 0).start()
 
+    turn(3, ws, wst)
     await_bytes(gat.at[lead, 0, 0, 0 : n - 1], r1.at[0])
     spread(0)
     await_bytes(gat.at[rest, 0, 0, 0 : n - 1], r1.at[1])
     for rel in range(1, NX):
         spread(rel)
 
-    for i in range(2, 6):
-        local[i].wait()
-    ones = (
-        lax.broadcasted_iota(jnp.int32, (LANES, LANES), 0) == lax.broadcasted_iota(jnp.int32, (LANES, LANES), 1)
-    ).astype(BF16)
-
-    def turn(i):
-        at = pl.ds(pl.multiple_of(i * LANES, LANES), LANES)
-        for src, dst in ((wt, wtt), (ws, wst)):
-            dst[at, :] = lax.dot_general(
-                ones, src[:, at], (((1,), (1,)), ((), ())), preferred_element_type=F32
-            ).astype(BF16)
-
-    each(width // LANES, turn, 0)
-
+    turn(2, wt, wtt)
+    local[4].wait()
+    local[5].wait()
     half = width // 2
     upper, lower = slice(0, half), slice(half, width)
 
@@ -170,18 +174,18 @@
                 swap(rel, d).start()
         await_bytes(gat.at[rel, 0], r3.at[rel])
 
-        def place(i):
-            a0, a1 = gat[rel, 0, i].astype(F32), gat[rel, 1, :, i].astype(F32)
+        columns = slice(rel * LANES, (rel + 1) * LANES)
+
+        def place(half_tile, dst, i):
+            halves = [gat[rel, 0, i].astype(F32)[:, half_tile], gat[rel, 1, :, i].astype(F32)[:, half_tile]]
             at = pl.ds(pl.multiple_of(i * (n * 16), n * 16), n * 16)
-            teacher = jnp.stack([a0[:, 0:8], a1[:, 0:8]], axis=1).reshape(n * 16, LANES)
-            student = jnp.stack([a0[:, 8:16], a1[:, 8:16]], axis=1).reshape(n * 16, LANES)
-            xt[at, :] = teacher.astype(BF16)
-            xs[at, rel * LANES : (rel + 1) * LANES] = student.astype(BF16)
-
-        each(n, place, 0)
-        student = jnp.dot(wst[...], xs[:, rel * LANES : (rel + 1) * LANES], preferred_element_type=F32)
+            dst[at] = jnp.stack(halves, axis=1).reshape(n * 16, LANES).astype(BF16)
+
+        each(n, functools.partial(place, slice(8, 16), xs.at[:, columns]), 0)
+        student = jnp.dot(wst[...], xs[:, columns], preferred_element_type=F32)
         part[rel, 1] = student
         after_student()
+        each(n, functools.partial(place, slice(0, 8), xt), 0)
         part[rel, 0] = student - jnp.dot(wtt[...], xt[...], preferred_element_type=F32)
         if rel == 0:
             diff[0], unit[0] = code(part[0, 0])
@@ -377,12 +381,11 @@
     g_rest[1].wait_recv()
     coef_copies[2].wait_recv()
     terms(1)
-    send_outer(2)
-    send_outer(1)
     await_bytes(gb.at[:, :, slot(0)], rg.at[6])
     coef_copies[0].wait_recv()
     terms(0)
-    send_outer(0)
+    for i in (2, 1, 0):
+        send_outer(i)
     await_bytes(lossb.at[0 : NX - 1], rs.at[2])
     loss = jnp.sum(lossb[:, 0:1].reshape(NX, LANES)) / rows
     loss_ref[...] = jnp.full((1, LANES), loss, F32)

time: 77.9 us -> 78.3 us (level)
  no operation moved by 1% of the time
where the time goes in v3:
time: 78.3 us; the launch traced here: 78.2 us
  Pallas kernels  77.5 us (99%)
    pallas_call x1, Pallas kernels, shards(): pl.pallas_call(functools.partial(kernel, n, rows), out_shape=(pltpu.VMEM(...  76.4 us

profile of v3, /device:TPU:1, one launch (start us, length us, event | category | flops | bytes accessed | tf_op | source)
XLA Modules:
  0.0 78.2 jit_solution(8208049454047470674)
XLA Ops:
  0.6 76.4 %shard_map.93 = (f32[1,128]{1,0:T(1,128)S(1)}, f32[1,128]{1,0:T(1,128)S(1)}, f32[8,512]{1,0:T(8,128)S(1)}, bf16[1024,640]{1,0:T(8,128)(2,1)S(1)}) custom-call(bf16[8,512]{1,0:T(8,128)(2,1)} %bitcast.7, bf16[8,512]{1,0:T(8,128)(2,1)} %bitcast.8, bf16[1024,640]{1,0:T(8,128)(2,1)} %wt_hbm.1, bf16[1024,640]{1,0:T(8,128)(2,1)} %ws_hbm.1, s32[1,128]{1,0:T(1,128)} %bitcast.10, ...), custom_call_target="tpu_custom_call" | custom-call | flops 6000000000 | bytes 5000000 | tf_op jit(solution)/shard_map/pallas_call | solution.py:482
  77.1 1.1 %shard_map.94 = (f32[1,128]{1,0:T(1,128)}, f32[1,1]{1,0:T(1,128)}, bf16[8,512]{1,0:T(8,128)(2,1)}, bf16[1024,640]{1,0:T(8,128)(2,1)}) custom-call(f32[1,128]{1,0:T(1,128)S(1)} %get-tuple-element.12.tok_ref, f32[1,128]{1,0:T(1,128)S(1)} %get-tuple-element.13.loss_ref, f32[8,512]{1,0:T(8,128)S(1)} %get-tuple-element.14.hid_ref, ...), custom_call_target="tpu_custom_call" | custom-call | tf_op jit(solution)/shard_map/pallas_call | solution.py:502
